TPU v7x, 32 devices: a whole 2x2x4 slice. The times are simulated.
32 devices in a mesh: seq: 8 (over y, x, core), head: 4 (over z).
Axes of the slice: x: 2, y: 2, z: 4, core: 2. Of those that a mesh axis runs over, the one named last changes fastest.
Arguments:
- cached_keys: bfloat16 [32768, 4096], P(('seq', 'head')), may hold values from -48 to 48
- sketch_matrix: bfloat16 [4096, 512], replicated, may hold values from -0.09375 to 0.09375
- cached_values: bfloat16 [32768, 4096], P('seq', 'head'), may hold values from -6 to 6
- queries: bfloat16 [8, 128, 128], P('head'), may hold values from -64 to 64
- new_keys: bfloat16 [4, 4096], P(None, 'head'), may hold values from -8.25 to 8.25
- new_values: bfloat16 [4, 4096], P(None, 'head'), may hold values from -6 to 6
Outputs:
- attended: bfloat16 [8, 128, 128], P('head', 'seq')
- key_bases: bfloat16 [32768, 512], P(('seq', 'head'))
- coefficients: bfloat16 [4096, 512], P('head')
All inputs are finite; a program needn't handle non-finite values.
Results may differ from a plain program's by a relative error of at most 0.01145.
The roundings to bfloat16 on the way count: a program that leaves them out, or rounds other values in their place, can miss the bound.
Values may be sent and summed in bfloat16 or wider, within the bound.
A program may use at most 128 MiB of HBM per device.

v0:
```python
import math

import jax
import jax.numpy as jnp
from jax import lax
from jax.sharding import PartitionSpec as P

GQA = 8
LAYERS = 4
STEPS = 4


def joined(part, axis, combine):
    gathered = jax.tree.map(lambda a: lax.all_gather(a, axis), part)

    def take(source):
        return jax.tree.map(lambda a: lax.dynamic_index_in_dim(a, source, 0, False), gathered)

    return lax.fori_loop(
        1, lax.axis_size(axis), lambda source, state: combine(state, take(source)), take(0)
    )


def right_solve(lower_factor, matrix):
    return lax.linalg.triangular_solve(
        lower_factor, matrix, left_side=False, lower=True, transpose_a=True
    )


def soft_join(former, latter):
    joint_peak = jnp.maximum(former[0], latter[0])
    former_factor = jnp.exp(former[0] - joint_peak)
    latter_factor = jnp.exp(latter[0] - joint_peak)
    return (
        joint_peak,
        former[1] * former_factor + latter[1] * latter_factor,
        former[2] * former_factor[..., None] + latter[2] * latter_factor[..., None],
    )


def per_device(cached_keys, sketch_matrix, cached_values, queries, new_keys, new_values):
    highest = lax.Precision.HIGHEST
    seq_count = lax.axis_size("seq")
    head_count = lax.axis_size("head")
    tok_rows, key_width = cached_keys.shape
    sketch_rank = sketch_matrix.shape[1]
    contract = (((0,), (0,)), ((), ()))
    sketch = jnp.dot(cached_keys, sketch_matrix, preferred_element_type=jnp.float32)
    gram_first = lax.psum(jnp.dot(sketch.T, sketch, precision=highest), ("seq", "head"))
    lower_first = jnp.linalg.cholesky(gram_first)
    orthonormal = right_solve(lower_first, sketch)
    stored_ortho = orthonormal.astype(jnp.bfloat16)
    sub_rows = key_width // (seq_count * head_count)
    arranged = (
        cached_keys.reshape(tok_rows, head_count, seq_count, sub_rows)
        .transpose(0, 2, 1, 3)
        .reshape(tok_rows, key_width)
    )
    coef_rows = lax.psum_scatter(
        lax.dot_general(arranged, stored_ortho, contract, preferred_element_type=jnp.float32),
        ("seq", "head"),
        scatter_dimension=0,
        tiled=True,
    )
    gram_second = lax.psum(jnp.dot(coef_rows.T, coef_rows, precision=highest), ("seq", "head"))
    lower_second = jnp.linalg.cholesky(gram_second)
    coef_piece = right_solve(lower_second, coef_rows).astype(jnp.bfloat16)
    coefficients = lax.all_gather(coef_piece, "seq", axis=0, tiled=True)
    key_bases = jnp.dot(orthonormal, lower_second, precision=highest).astype(jnp.bfloat16)
    heads_here, query_rows, head_dim = queries.shape
    rows_layer = STEPS * GQA
    score_scale = 1.0 / math.sqrt(head_dim)
    query_view = queries.reshape(heads_here, LAYERS, rows_layer, head_dim)
    coef_view = coefficients.reshape(heads_here, LAYERS, head_dim, sketch_rank)
    absorbed = (
        jnp.einsum("klqh,klhr->klqr", query_view, coef_view, preferred_element_type=jnp.float32)
        * score_scale
    ).astype(jnp.bfloat16)
    flat_queries = absorbed.reshape(heads_here * query_rows, sketch_rank)
    cache_scores = lax.dot_general(
        flat_queries,
        lax.all_gather(key_bases, "head", axis=0, tiled=True),
        (((1,), (1,)), ((), ())),
        preferred_element_type=jnp.float32,
    )
    local_peak = jnp.max(cache_scores, axis=1)
    cache_weights = jnp.exp(cache_scores - local_peak[:, None])
    local_total = jnp.sum(cache_weights, axis=1)
    weights_bf = cache_weights.astype(jnp.bfloat16).reshape(heads_here, LAYERS, rows_layer, -1)
    value_view = cached_values.reshape(cached_values.shape[0], heads_here, LAYERS, head_dim)
    numerator = jnp.einsum(
        "klqn,nklh->klqh", weights_bf, value_view, preferred_element_type=jnp.float32
    ).reshape(heads_here, query_rows, head_dim)
    row_peaks = local_peak.reshape(heads_here, query_rows)
    totals = local_total.reshape(heads_here, query_rows)
    own_rows = query_rows // seq_count
    row_begin = lax.axis_index("seq") * own_rows
    row_peaks, totals, numerator = joined((row_peaks, totals, numerator), "seq", soft_join)
    row_peaks = lax.dynamic_slice_in_dim(row_peaks, row_begin, own_rows, 1)
    totals = lax.dynamic_slice_in_dim(totals, row_begin, own_rows, 1)
    numerator = lax.dynamic_slice_in_dim(numerator, row_begin, own_rows, 1)
    row_index = row_begin + jnp.arange(own_rows, dtype=jnp.int32)
    layer_of_row = row_index // rows_layer
    step_of_row = row_index // GQA % STEPS
    layer_pick = (layer_of_row[:, None] == jnp.arange(LAYERS, dtype=jnp.int32)[None, :]).astype(
        jnp.float32
    )
    allowed = step_of_row[:, None] >= jnp.arange(STEPS, dtype=jnp.int32)[None, :]
    own_queries = lax.dynamic_slice_in_dim(queries, row_begin, own_rows, 1)
    fresh_keys = new_keys.reshape(STEPS, heads_here, LAYERS, head_dim)
    fresh_all = (
        jnp.einsum("kqh,uklh->kqul", own_queries, fresh_keys, preferred_element_type=jnp.float32)
        * score_scale
    )
    fresh_scores = jnp.sum(fresh_all * layer_pick[None, :, None, :], axis=3)
    fresh_scores = jnp.where(allowed[None], fresh_scores, -jnp.inf)
    overall = jnp.maximum(row_peaks, jnp.max(fresh_scores, axis=2))
    cache_factor = jnp.exp(row_peaks - overall)
    fresh_weights = jnp.exp(fresh_scores - overall[..., None])
    fresh_vals = jnp.transpose(
        new_values.astype(jnp.float32).reshape(STEPS, heads_here, LAYERS, head_dim), (1, 0, 2, 3)
    )
    picked = jnp.sum(layer_pick[None, :, None, :, None] * fresh_vals[:, None], axis=3)
    fresh_part = jnp.sum(fresh_weights[..., None] * picked, axis=2)
    softmax_total = totals * cache_factor + jnp.sum(fresh_weights, axis=2)
    attended = (
        (numerator * cache_factor[..., None] + fresh_part) / softmax_total[..., None]
    ).astype(jnp.bfloat16)
    return (attended, key_bases, coefficients)


def solution(mesh):
    placed = (
        P(("seq", "head"), None),
        P(),
        P("seq", "head"),
        P("head", None, None),
        P(None, "head"),
        P(None, "head"),
    )
    return jax.shard_map(
        per_device,
        mesh=mesh,
        in_specs=placed,
        out_specs=(P("head", "seq", None), P(("seq", "head"), None), P("head", None)),
        check_vma=False,
    )
```

profile of v0, /device:TPU:0, one launch (start us, length us, event | category | flops | bytes accessed | tf_op | source)
XLA Modules:
  0.0 948.1 jit_solution(13541112434446647214)
XLA Ops:
  7.2 8.1 fusion.101
  20.0 12.1 %copy.62 = bf16[1024,4096]{0,1:T(8,128)(2,1)} copy(bf16[1024,4096]{1,0:T(8,128)(2,1)} %param.9) | data formatting | bytes 16777216 | tf_op args[0]
  32.1 8.2 copy.63
  40.3 112.3 %all-reduce.4.cloned.1.call-done = f32[512,512]{0,1:T(8,128)} async-done(((f32[512,512]{0,1:T(8,128)}), f32[512,512]{0,1:T(8,128)}) %all-reduce.4.cloned.1.call-update) | async-done | bytes 1048592 | tf_op jit(solution)/shard_map/psum | solution.py:49
  157.9 11.7 %cholesky.286 = f32[128,128]{1,0:T(8,128)S(1)} custom-call(f32[128,128]{1,0:T(8,128)S(1)} %cholesky.426), custom_call_target="Cholesky" | custom-call | tf_op jit(solution)/shard_map/jit(cholesky)/cholesky | solution.py:50
  169.7 9.8 %custom-call.31 = f32[1,128,128]{1,2,0:T(8,128)S(1)} custom-call(f32[1,128,128]{2,1,0:T(8,128)S(1)} %get-tuple-element.279), custom_call_target="InvertDiagBlocksLowerTriangular" | custom-call | tf_op jit(solution)/shard_map/jit(cholesky)/cholesky | solution.py:50
  183.8 11.7 %cholesky.305 = f32[128,128]{1,0:T(8,128)S(1)} custom-call(f32[128,128]{1,0:T(8,128)S(1)} %cholesky.430), custom_call_target="Cholesky" | custom-call | tf_op jit(solution)/shard_map/jit(cholesky)/cholesky | solution.py:50
  196.1 10.1 %custom-call.32 = f32[1,128,128]{1,2,0:T(8,128)S(1)} custom-call(f32[1,128,128]{2,1,0:T(8,128)S(1)} %get-tuple-element.276), custom_call_target="InvertDiagBlocksLowerTriangular" | custom-call | tf_op jit(solution)/shard_map/jit(cholesky)/cholesky | solution.py:50
  208.6 11.7 %cholesky.326 = f32[128,128]{1,0:T(8,128)S(1)} custom-call(f32[128,128]{1,0:T(8,128)S(1)} %cholesky.435), custom_call_target="Cholesky" | custom-call | tf_op jit(solution)/shard_map/jit(cholesky)/cholesky | solution.py:50
  221.6 9.8 %custom-call.33 = f32[1,128,128]{1,2,0:T(8,128)S(1)} custom-call(f32[1,128,128]{2,1,0:T(8,128)S(1)} %get-tuple-element.273), custom_call_target="InvertDiagBlocksLowerTriangular" | custom-call | tf_op jit(solution)/shard_map/jit(cholesky)/cholesky | solution.py:50
  233.6 11.9 %cholesky.343 = f32[128,128]{1,0:T(8,128)S(1)} custom-call(f32[128,128]{1,0:T(8,128)S(1)} %convolution_subtract_fusion.10), custom_call_target="Cholesky" | custom-call | tf_op jit(solution)/shard_map/jit(cholesky)/cholesky | solution.py:50
  252.2 11.3 %while.22 = (s32[]{:T(128)}, f32[512,512]{1,0:T(8,128)}, s32[4,2]{0,1:T(2,128)S(1)}, f32[4,128,128]{2,1,0:T(8,128)S(1)}, s32[]{:T(128)}) while((s32[]{:T(128)}, f32[512,512]{1,0:T(8,128)}, s32[4,2]{0,1:T(2,128)S(1)}, f32[4,128,128]{2,1,0:T(8,128)S(1)}, s32[]{:T(128)}) %tuple.102), condition=%wide.while_cond, body=%wide.while_body.sunk | while | flops 2 | bytes 131181 | solution.py:25
  263.5 39.3 %custom-call.26 = f32[4,128,128]{1,2,0:T(8,128)S(1)} custom-call(f32[4,128,128]{2,1,0:T(8,128)S(1)} %get-tuple-element.192), custom_call_target="InvertDiagBlocksLowerTriangular" | custom-call | tf_op jit(solution)/shard_map/triangular_solve | solution.py:25
  313.8 10.6 %convolution_bitcast_fusion = f32[4096,512]{0,1:T(8,128)} fusion(bf16[1024,4096]{0,1:T(8,128)(2,1)} %bitcast.165, f32[1024,128]{0,1:T(8,128)S(1)} %fusion.62, f32[1024,128]{0,1:T(8,128)S(1)} %fusion.63, f32[1024,128]{0,1:T(8,128)S(1)} %fusion.64, f32[1024,128]{0,1:T(8,128)S(1)} %fusion.26), kind=kOutput, calls=%fused_computation.15 | convolution fusion | flops 4299161600 | bytes 18874368 | tf_op jit(solution)/shard_map/dot_general | solution.py:60
  324.5 184.9 %reduce-scatter.2.cloned.1.call-done = f32[128,512]{0,1:T(8,128)} async-done(((f32[4096,512]{0,1:T(8,128)}), f32[128,512]{0,1:T(8,128)}) %reduce-scatter.2.cloned.1.call-update) | async-done | bytes 262160 | tf_op jit(solution)/shard_map/reduce_scatter | solution.py:59
  512.8 130.7 %all-reduce.6.cloned.1.call-done = f32[512,512]{0,1:T(8,128)} async-done(((f32[512,512]{0,1:T(8,128)}), f32[512,512]{0,1:T(8,128)}) %all-reduce.6.cloned.1.call-update) | async-done | bytes 1048592 | tf_op jit(solution)/shard_map/psum | solution.py:65
  646.4 11.7 %cholesky.358 = f32[128,128]{1,0:T(8,128)S(1)} custom-call(f32[128,128]{1,0:T(8,128)S(1)} %cholesky.439), custom_call_target="Cholesky" | custom-call | tf_op jit(solution)/shard_map/jit(cholesky)/cholesky | solution.py:66
  658.3 9.8 %custom-call.34 = f32[1,128,128]{1,2,0:T(8,128)S(1)} custom-call(f32[1,128,128]{2,1,0:T(8,128)S(1)} %get-tuple-element.269), custom_call_target="InvertDiagBlocksLowerTriangular" | custom-call | tf_op jit(solution)/shard_map/jit(cholesky)/cholesky | solution.py:66
  670.6 11.7 %cholesky.377 = f32[128,128]{1,0:T(8,128)S(1)} custom-call(f32[128,128]{1,0:T(8,128)S(1)} %cholesky.443), custom_call_target="Cholesky" | custom-call | tf_op jit(solution)/shard_map/jit(cholesky)/cholesky | solution.py:66
  683.7 9.9 %custom-call.35 = f32[1,128,128]{1,2,0:T(8,128)S(1)} custom-call(f32[1,128,128]{2,1,0:T(8,128)S(1)} %get-tuple-element.266), custom_call_target="InvertDiagBlocksLowerTriangular" | custom-call | tf_op jit(solution)/shard_map/jit(cholesky)/cholesky | solution.py:66
  695.2 11.7 %cholesky.398 = f32[128,128]{1,0:T(8,128)S(1)} custom-call(f32[128,128]{1,0:T(8,128)S(1)} %cholesky.448), custom_call_target="Cholesky" | custom-call | tf_op jit(solution)/shard_map/jit(cholesky)/cholesky | solution.py:66
  707.6 9.8 %custom-call.36 = f32[1,128,128]{1,2,0:T(8,128)S(1)} custom-call(f32[1,128,128]{2,1,0:T(8,128)S(1)} %get-tuple-element.263), custom_call_target="InvertDiagBlocksLowerTriangular" | custom-call | tf_op jit(solution)/shard_map/jit(cholesky)/cholesky | solution.py:66
  718.9 11.7 %cholesky.415 = f32[128,128]{1,0:T(8,128)S(1)} custom-call(f32[128,128]{1,0:T(8,128)S(1)} %convolution_subtract_fusion.9), custom_call_target="Cholesky" | custom-call | tf_op jit(solution)/shard_map/jit(cholesky)/cholesky | solution.py:66
  734.9 10.9 %while.23 = (s32[]{:T(128)}, f32[512,512]{1,0:T(8,128)S(1)}, s32[4,2]{0,1:T(2,128)S(1)}, f32[4,128,128]{2,1,0:T(8,128)}, s32[]{:T(128)}) while((s32[]{:T(128)}, f32[512,512]{1,0:T(8,128)S(1)}, s32[4,2]{0,1:T(2,128)S(1)}, f32[4,128,128]{2,1,0:T(8,128)}, s32[]{:T(128)}) %tuple.123), condition=%wide.while_cond.1, body=%wide.while_body.1.sunk | while | flops 2 | bytes 132705 | solution.py:25
  745.8 40.8 %custom-call.27 = f32[4,128,128]{1,2,0:T(8,128)} custom-call(f32[4,128,128]{2,1,0:T(8,128)} %get-tuple-element.200), custom_call_target="InvertDiagBlocksLowerTriangular" | custom-call | tf_op jit(solution)/shard_map/triangular_solve | solution.py:25
  792.7 5.7 convolution_convert_fusion
  798.7 14.3 %reshape.193 = bf16[4096,2,4,128]{3,2,1,0:T(4,128)(2,1)} reshape(bf16[4096,1024]{1,0:T(8,128)(2,1)} %param.11) | data formatting | bytes 16777216 | tf_op jit(solution)/shard_map/reshape | solution.py:90
  817.1 81.0 %all-gather.6.cloned.1.call-done = bf16[4096,512]{1,0:T(8,128)(2,1)} async-done(((bf16[1024,512]{1,0:T(8,128)(2,1)}), bf16[4096,512]{1,0:T(8,128)(2,1)}) %all-gather.6.cloned.1.call-update) | async-done | bytes 4194320 | tf_op jit(solution)/shard_map/all_gather | solution.py:82
  902.5 6.6 fusion.3
  909.4 8.9 all_gather.18
  918.3 8.8 all_gather.17
  932.1 7.8 while.21
  (155 shorter events, 102.5 us)
Async XLA Ops:
  7.2 809.7 %copy-start = (bf16[2,128,128]{2,1,0:T(8,128)(2,1)S(1)}, bf16[2,128,128]{2,1,0:T(8,128)(2,1)}, u32[]{:S(2)}) copy-start(bf16[2,128,128]{2,1,0:T(8,128)(2,1)} %param.12) | copy-start | bytes 196612
  7.2 145.4 %all-reduce.4.cloned.1.call-start = ((), (), s32[]{:S(2)}) async-start(), calls=%async_computation.1 | async-start | bytes 2097152 | tf_op jit(solution)/shard_map/psum | solution.py:49
  19.9 489.4 %reduce-scatter.2.cloned.1.call-start = ((), (), s32[]{:S(2)}) async-start(), calls=%async_computation.2 | async-start | bytes 8650752 | tf_op jit(solution)/shard_map/reduce_scatter | solution.py:59
  156.9 1.0 copy-start.4
  309.2 4.5 copy-start.6
  313.8 10.6 %copy-start.7 = (f32[1024,128]{0,1:T(8,128)}, f32[1024,128]{0,1:T(8,128)S(1)}, u32[]{:S(2)}) copy-start(f32[1024,128]{0,1:T(8,128)S(1)} %fusion.62) | copy-start | bytes 1572868
  324.4 319.1 %all-reduce.6.cloned.1.call-start = ((), (), s32[]{:S(2)}) async-start(), calls=%async_computation.3 | async-start | bytes 2097152 | tf_op jit(solution)/shard_map/psum | solution.py:65
  512.4 303.0 %all-gather.4.cloned.1.call-start = ((), (), s32[]{:S(2)}) async-start(), calls=%async_computation.4 | async-start | bytes 1179648 | tf_op jit(solution)/shard_map/all_gather | solution.py:68
  643.5 1.7 copy-start.1
  645.4 1.0 copy-start.3
  695.2 91.3 %copy-start.5 = (f32[128,512]{0,1:T(8,128)S(1)}, f32[128,512]{0,1:T(8,128)}, u32[]{:S(2)}) copy-start(f32[128,512]{0,1:T(8,128)} %reduce-scatter.2.cloned.1.call-done) | copy-start | bytes 786436
  792.6 105.5 %all-gather.6.cloned.1.call-start = ((), (), s32[]{:S(2)}) async-start(), calls=%async_computation.5 | async-start | bytes 5242880 | tf_op jit(solution)/shard_map/all_gather | solution.py:82
  798.4 132.8 %all-gather.8.cloned.1.call-start = ((), (), s32[]{:S(2)}) async-start(), calls=%async_computation.6 | async-start | bytes 1179648 | tf_op jit(solution)/shard_map/all_gather | solution.py:14
  816.8 84.8 %copy-start.2 = (bf16[1024,512]{1,0:T(8,128)(2,1)}, bf16[1024,512]{1,0:T(8,128)(2,1)S(1)}, u32[]{:S(2)}) copy-start(bf16[1024,512]{1,0:T(8,128)(2,1)S(1)} %copy.80) | copy-start | bytes 3145732
  902.4 6.6 copy-start.9
  902.4 6.6 copy-start.8
Sparse Core Ops, SparseCore 0:
  20.0 132.5 all-reduce.3
  324.5 184.7 reduce-scatter.1
  515.9 127.5 all-reduce.5
  792.7 22.5 all-gather.3
  817.3 80.7 all-gather.5
  909.2 22.0 all-gather.7
where the time goes:
time: 954 us; the launch traced here: 948 us
  waiting for transfers between devices  515 us (54%)
  other arithmetic  255 us (27%)
  matrix products  71.9 us (8%)
  local copies, waits for them, and re-layouts  67.3 us (7%)
  between operations  19.9 us (2%)
  blocking collectives  17.7 us (2%)
    reduce_scatter x1, waiting for transfers between devices, per_device(): lax.psum_scatter(lax.dot_general(arranged, stored_ortho, contract, prefer...  185 us
    psum x1, waiting for transfers between devices, per_device(): lax.psum(jnp.dot(coef_rows.T, coef_rows, precision=highest), ('seq', 'hea...  131 us
    psum x1, waiting for transfers between devices, per_device(): lax.psum(jnp.dot(sketch.T, sketch, precision=highest), ('seq', 'head'))  112 us
    another operation x6, other arithmetic, right_solve(): lax.linalg.triangular_solve(lower_factor, matrix, left_side=False, lower=...  83.4 us
    all_gather x1, waiting for transfers between devices, per_device(): lax.all_gather(key_bases, 'head', axis=0, tiled=True)  81 us
    another operation x14, other arithmetic, per_device(): lower_first = jnp.linalg.cholesky(gram_first)  80.6 us
    another operation x15, other arithmetic, per_device(): lower_second = jnp.linalg.cholesky(gram_second)  79.2 us
    another operation x24, local copies, waits for them, and re-layouts  22.1 us
  transfers between devices with their start and end apart: 6, of which 6 were waited for; matrix products, arithmetic and copies ran while one was open for 4% of the time, Pallas kernels for 0%

commit v1 on v0

--- a/solution.py
+++ b/solution.py
@@ -1,13 +1,84 @@
+import functools
 import math
 
 import jax
 import jax.numpy as jnp
 from jax import lax
+from jax.experimental import pallas as pl
+from jax.experimental.pallas import tpu as pltpu
 from jax.sharding import PartitionSpec as P
 
 GQA = 8
 LAYERS = 4
 STEPS = 4
+HI = lax.Precision.HIGHEST
+BLK = 128
+
+def eliminate(square):
+    groups = BLK // 8
+    sub = lax.broadcasted_iota(jnp.int32, (8, BLK), 0)
+    lane = lax.broadcasted_iota(jnp.int32, (8, BLK), 1)
+    s = [square[8 * g:8 * g + 8, :] for g in range(groups)]
+    w = [(lane == sub + 8 * g).astype(jnp.float32) for g in range(groups)]
+    for j in range(BLK):
+        gj, r = divmod(j, 8)
+        row = s[gj][r:r + 1, :]
+        inv = 1.0 / jnp.broadcast_to(row[:, j:j + 1], (1, BLK))
+        srow = jnp.broadcast_to(row * inv, (8, BLK))
+        wrow = jnp.broadcast_to(w[gj][r:r + 1, :] * inv, (8, BLK))
+        for g in range(gj, groups):
+            if g == gj and r == 7:
+                continue
+            col = jnp.broadcast_to(s[g][:, j:j + 1], (8, BLK))
+            if g == gj:
+                col = jnp.where(sub > r, col, 0.0)
+            s[g] = s[g] - col * srow
+            w[g] = w[g] - col * wrow
+    out = []
+    for g in range(groups):
+        diag = jnp.sum(jnp.where(lane == sub + 8 * g, s[g], 0.0), axis=1, keepdims=True)
+        out.append(w[g] * lax.rsqrt(diag))
+    return jnp.concatenate(out, axis=0)
+
+def factor(mat, size):
+    n = size // BLK
+    lane = lax.broadcasted_iota(jnp.int32, (BLK, 2 * size), 1)
+
+    def panel(k, carry):
+        r0 = pl.multiple_of(k * BLK, BLK)
+        inv = eliminate(mat[pl.ds(r0, BLK), pl.ds(r0, BLK)])
+        solved = jnp.dot(inv, mat[pl.ds(r0, BLK), :], precision=HI, preferred_element_type=jnp.float32)
+        mat[pl.ds(r0, BLK), :] = jnp.where(lane >= r0, solved, 0.0)
+
+        def below(i, c):
+            i0 = pl.multiple_of(i * BLK, BLK)
+            mat[pl.ds(i0, BLK), :] -= lax.dot_general(
+                mat[pl.ds(r0, BLK), pl.ds(i0, BLK)], mat[pl.ds(r0, BLK), :],
+                (((0,), (0,)), ((), ())), precision=HI, preferred_element_type=jnp.float32)
+            return c
+        lax.fori_loop(k + 1, n, below, 0)
+        return carry
+    lax.fori_loop(0, n, panel, 0)
+
+def kernel(size, g_ref, u_ref, v_ref, mat):
+    r = lax.broadcasted_iota(jnp.int32, (size, size), 0)
+    c = lax.broadcasted_iota(jnp.int32, (size, size), 1)
+    mat[:, :size] = g_ref[...]
+    mat[:, size:] = (r == c).astype(jnp.float32)
+    factor(mat, size)
+    u_ref[...] = jnp.where(c >= r, mat[:, :size], 0.0)
+    v_ref[...] = mat[:, size:]
+
+def chol_inv(g):
+    size = g.shape[0]
+    return pl.pallas_call(
+        functools.partial(kernel, size),
+        out_shape=[jax.ShapeDtypeStruct((size, size), jnp.float32)] * 2,
+        in_specs=[pl.BlockSpec(memory_space=pltpu.VMEM)],
+        out_specs=[pl.BlockSpec(memory_space=pltpu.VMEM)] * 2,
+        scratch_shapes=[pltpu.VMEM((size, 2 * size), jnp.float32)],
+        compiler_params=pltpu.CompilerParams(vmem_limit_bytes=32 << 20),
+    )(g)
 
 
 def joined(part, axis, combine):
@@ -18,12 +89,6 @@
 
     return lax.fori_loop(
         1, lax.axis_size(axis), lambda source, state: combine(state, take(source)), take(0)
-    )
-
-
-def right_solve(lower_factor, matrix):
-    return lax.linalg.triangular_solve(
-        lower_factor, matrix, left_side=False, lower=True, transpose_a=True
     )
 
 
@@ -47,26 +112,25 @@
     contract = (((0,), (0,)), ((), ()))
     sketch = jnp.dot(cached_keys, sketch_matrix, preferred_element_type=jnp.float32)
     gram_first = lax.psum(jnp.dot(sketch.T, sketch, precision=highest), ("seq", "head"))
-    lower_first = jnp.linalg.cholesky(gram_first)
-    orthonormal = right_solve(lower_first, sketch)
+    _, inverse_first = chol_inv(gram_first)
+    rows_with_rows = (((1,), (1,)), ((), ()))
+    orthonormal = lax.dot_general(sketch, inverse_first, rows_with_rows, precision=highest)
     stored_ortho = orthonormal.astype(jnp.bfloat16)
-    sub_rows = key_width // (seq_count * head_count)
-    arranged = (
-        cached_keys.reshape(tok_rows, head_count, seq_count, sub_rows)
-        .transpose(0, 2, 1, 3)
-        .reshape(tok_rows, key_width)
-    )
     coef_rows = lax.psum_scatter(
-        lax.dot_general(arranged, stored_ortho, contract, preferred_element_type=jnp.float32),
-        ("seq", "head"),
+        lax.dot_general(cached_keys, stored_ortho, contract, preferred_element_type=jnp.float32),
+        ("head", "seq"),
         scatter_dimension=0,
         tiled=True,
     )
     gram_second = lax.psum(jnp.dot(coef_rows.T, coef_rows, precision=highest), ("seq", "head"))
-    lower_second = jnp.linalg.cholesky(gram_second)
-    coef_piece = right_solve(lower_second, coef_rows).astype(jnp.bfloat16)
+    upper_second, inverse_second = chol_inv(gram_second)
+    coef_piece = lax.dot_general(
+        coef_rows, inverse_second, rows_with_rows, precision=highest
+    ).astype(jnp.bfloat16)
     coefficients = lax.all_gather(coef_piece, "seq", axis=0, tiled=True)
-    key_bases = jnp.dot(orthonormal, lower_second, precision=highest).astype(jnp.bfloat16)
+    key_bases = lax.dot_general(
+        orthonormal, upper_second, rows_with_rows, precision=highest
+    ).astype(jnp.bfloat16)
     heads_here, query_rows, head_dim = queries.shape
     rows_layer = STEPS * GQA
     score_scale = 1.0 / math.sqrt(head_dim)

time: 954 us -> 707 us (0.74)
  other arithmetic: 255 us -> 9.54 us
  Pallas kernels: 0 us -> 98.8 us
  local copies, waits for them, and re-layouts: 67.3 us -> 20.2 us
  matrix products: 71.9 us -> 46.7 us
  waiting for transfers between devices: 515 us -> 498 us
    another operation x35 -> x0, other arithmetic: 243 us -> none  [the longest x6 83.4 us: right_solve(): lax.linalg.triangular_solve(lower_factor, matrix, left_side=False, lower=...]
    pallas_call x0 -> x2, Pallas kernels: none -> 98.8 us  [chol_inv(): pl.pallas_call(functools.partial(kernel, size), out_shape=[jax.ShapeDtype...]
    reduce_scatter x1, waiting for transfers between devices: 185 us -> 148 us  [per_device(): lax.psum_scatter(lax.dot_general(cached_keys, stored_ortho, contract, pre...]
    another operation x26 -> x0, matrix products: 29.5 us -> none  [the longest x14 16.2 us: right_solve(): lax.linalg.triangular_solve(lower_factor, matrix, left_side=False, lower=...]
    another operation x33 -> x0, local copies, waits for them, and re-layouts: 23.4 us -> none
    psum x1, waiting for transfers between devices: 112 us -> 132 us  [per_device(): lax.psum(jnp.dot(sketch.T, sketch, precision=highest), ('seq', 'head'))]
    unnamed x23 -> x17, local copies, waits for them, and re-layouts: 14.8 us -> 4.93 us
    dot_general x2 -> x4, matrix products: 16.3 us -> 22.5 us  [the longest x1 10.2 us: per_device(): lax.dot_general(cached_keys, stored_ortho, contract, preferred_element_ty...]
  transfers between devices with their start and end apart: 6 -> 6, of which waited for: 6 -> 6; matrix products, arithmetic and copies ran while one was open for 4% -> 3% of each run, Pallas kernels for 0% -> 0%
where the time goes in v1:
time: 707 us; the launch traced here: 706 us
  waiting for transfers between devices  498 us (70%)
  Pallas kernels  98.8 us (14%)
  matrix products  46.7 us (7%)
  local copies, waits for them, and re-layouts  20.2 us (3%)
  blocking collectives  17.7 us (3%)
  between operations  14.2 us (2%)
  other arithmetic  9.54 us (1%)
    reduce_scatter x1, waiting for transfers between devices, per_device(): lax.psum_scatter(lax.dot_general(cached_keys, stored_ortho, contract, pre...  148 us
    psum x1, waiting for transfers between devices, per_device(): lax.psum(jnp.dot(sketch.T, sketch, precision=highest), ('seq', 'head'))  132 us
    psum x1, waiting for transfers between devices, per_device(): lax.psum(jnp.dot(coef_rows.T, coef_rows, precision=highest), ('seq', 'hea...  129 us
    pallas_call x2, Pallas kernels, chol_inv(): pl.pallas_call(functools.partial(kernel, size), out_shape=[jax.ShapeDtype...  98.8 us
    all_gather x1, waiting for transfers between devices, per_device(): lax.all_gather(key_bases, 'head', axis=0, tiled=True)  81.3 us
    all_gather x2, blocking collectives, joined(): gathered = jax.tree.map(lambda a: lax.all_gather(a, axis), part)  17.7 us
    reshape x1, local copies, waits for them, and re-layouts, per_device(): cached_values.reshape(cached_values.shape[0], heads_here, LAYERS, head_dim)  14.3 us
  transfers between devices with their start and end apart: 6, of which 6 were waited for; matrix products, arithmetic and copies ran while one was open for 3% of the time, Pallas kernels for 0%

profile of v1, /device:TPU:0, one launch (start us, length us, event | category | flops | bytes accessed | tf_op | source)
XLA Modules:
  0.0 706.3 jit_solution(12380457544575211101)
XLA Ops:
  7.2 8.2 %fusion.22 = f32[1024,512]{1,0:T(8,128)S(1)} fusion(bf16[1024,4096]{1,0:T(8,128)(2,1)} %param.8, bf16[4096,512]{1,0:T(8,128)(2,1)} %param.9), kind=kOutput, calls=%fused_computation.57 | convolution fusion | flops 4294967296 | bytes 14680064 | tf_op jit(solution)/shard_map/dot_general | solution.py:113
  15.4 1.3 copy-done.3
  16.7 4.5 fusion.23
  21.5 132.4 %all-reduce.3.cloned.1.call-done.g_ref = f32[512,512]{1,0:T(8,128)} async-done(((f32[512,512]{1,0:T(8,128)}), f32[512,512]{1,0:T(8,128)}) %all-reduce.3.cloned.1.call-update) | async-done | bytes 1048592 | tf_op jit(solution)/shard_map/psum | solution.py:114
  153.9 1.2 copy-done.1
  155.1 49.9 %shard_map.85 = (f32[512,512]{1,0:T(8,128)}, f32[512,512]{1,0:T(8,128)S(1)}) custom-call(f32[512,512]{1,0:T(8,128)S(1)} %copy-done.1), custom_call_target="tpu_custom_call" | custom-call | tf_op jit(solution)/shard_map/pallas_call | solution.py:74
  205.0 5.0 fusion.24
  210.0 10.2 %convolution_bitcast_fusion = f32[4096,512]{0,1:T(8,128)} fusion(bf16[1024,4096]{1,0:T(8,128)(2,1)} %param.8, f32[1024,512]{1,0:T(8,128)S(1)} %fusion.24), kind=kOutput, calls=%fused_computation.11 | convolution fusion | flops 4295491584 | bytes 18874368 | tf_op jit(solution)/shard_map/dot_general | solution.py:120
  220.3 147.7 %reduce-scatter.2.cloned.1.call-done = f32[128,512]{0,1:T(8,128)} async-done(((f32[4096,512]{0,1:T(8,128)}), f32[128,512]{0,1:T(8,128)}) %reduce-scatter.2.cloned.1.call-update) | async-done | bytes 262160 | tf_op jit(solution)/shard_map/reduce_scatter | solution.py:119
  368.0 3.0 fusion.25
  371.2 129.1 %all-reduce.5.cloned.1.call-done.g_ref = f32[512,512]{1,0:T(8,128)} async-done(((f32[512,512]{1,0:T(8,128)}), f32[512,512]{1,0:T(8,128)}) %all-reduce.5.cloned.1.call-update) | async-done | bytes 1048592 | tf_op jit(solution)/shard_map/psum | solution.py:125
  500.3 1.2 copy-done.2
  501.5 48.9 %shard_map.86 = (f32[512,512]{1,0:T(8,128)S(1)}, f32[512,512]{1,0:T(8,128)S(1)}) custom-call(f32[512,512]{1,0:T(8,128)S(1)} %copy-done.2), custom_call_target="tpu_custom_call" | custom-call | tf_op jit(solution)/shard_map/pallas_call | solution.py:74
  550.5 2.9 convolution_convert_fusion.1
  553.4 4.4 convolution_convert_fusion
  558.2 14.3 %reshape.146 = bf16[4096,2,4,128]{3,2,1,0:T(4,128)(2,1)} reshape(bf16[4096,1024]{1,0:T(8,128)(2,1)} %param.10) | data formatting | bytes 16777216 | tf_op jit(solution)/shard_map/reshape | solution.py:154
  572.5 3.5 all-gather.4.cloned.1.call-done
  576.0 1.5 fusion.7
  577.5 81.3 %all-gather.6.cloned.1.call-done = bf16[4096,512]{1,0:T(8,128)(2,1)} async-done(((bf16[1024,512]{1,0:T(8,128)(2,1)}), bf16[4096,512]{1,0:T(8,128)(2,1)}) %all-gather.6.cloned.1.call-update) | async-done | bytes 4194320 | tf_op jit(solution)/shard_map/all_gather | solution.py:146
  658.8 3.7 fusion.21
  663.4 3.2 fusion.3
  667.0 8.9 %all_gather.18 = f32[8,2,128]{2,1,0:T(2,128)S(1)} all-gather(f32[1,2,128]{2,1,0:T(2,128)S(1)} %bitcast.69), channel_id=1, replica_groups=mesh['seq'=8,'head'=4] {'seq'}, dimensions={0}, use_global_device_ids=true | all-gather | bytes 9216 | tf_op jit(solution)/shard_map/all_gather | solution.py:85
  675.9 8.8 %all_gather.17 = f32[8,2,128]{2,1,0:T(2,128)S(1)} all-gather(f32[1,2,128]{2,1,0:T(2,128)S(1)} %bitcast.68), channel_id=1, replica_groups=mesh['seq'=8,'head'=4] {'seq'}, dimensions={0}, use_global_device_ids=true | all-gather | bytes 9216 | tf_op jit(solution)/shard_map/all_gather | solution.py:85
  684.7 4.1 all-gather.8.cloned.1.call-done
  689.7 7.8 %while.19 = (s32[]{:T(128)}, f32[2,128]{1,0:T(2,128)S(1)}, f32[2,128]{1,0:T(2,128)S(1)}, f32[2,128,128]{2,1,0:T(8,128)S(1)}, f32[8,2,128]{2,1,0:T(2,128)S(1)}, /...) while((s32[]{:T(128)}, f32[2,128]{1,0:T(2,128)S(1)}, ...), condition=%wide.region_6.7_spmd, body=%wide.region_5.6_spmd.sunk | while | flops 99845 | bytes 403607 | solution.py:90
  689.7 1.1 fusion.49
  690.9 1.1 fusion.49
  692.0 1.1 fusion.49
  693.1 1.1 fusion.49
  694.2 1.1 fusion.49
  695.4 1.1 fusion.49
  696.5 1.1 fusion.49
  (51 shorter events, 5.3 us)
Async XLA Ops:
  7.2 568.8 %copy-start = (bf16[2,128,128]{2,1,0:T(8,128)(2,1)S(1)}, bf16[2,128,128]{2,1,0:T(8,128)(2,1)}, u32[]{:S(2)}) copy-start(bf16[2,128,128]{2,1,0:T(8,128)(2,1)} %param.11) | copy-start | bytes 196612
  7.2 146.7 %all-reduce.3.cloned.1.call-start = ((), (), s32[]{:S(2)}) async-start(), calls=%async_computation.1 | async-start | bytes 2097152 | tf_op jit(solution)/shard_map/psum | solution.py:114
  15.4 1.3 copy-start.3
  21.2 346.7 %reduce-scatter.2.cloned.1.call-start = ((), (), s32[]{:S(2)}) async-start(), calls=%async_computation.2 | async-start | bytes 8650752 | tf_op jit(solution)/shard_map/reduce_scatter | solution.py:119
  153.9 1.2 copy-start.1
  220.2 280.1 %all-reduce.5.cloned.1.call-start = ((), (), s32[]{:S(2)}) async-start(), calls=%async_computation.3 | async-start | bytes 2097152 | tf_op jit(solution)/shard_map/psum | solution.py:125
  371.0 205.0 %all-gather.4.cloned.1.call-start = ((), (), s32[]{:S(2)}) async-start(), calls=%async_computation.4 | async-start | bytes 1179648 | tf_op jit(solution)/shard_map/all_gather | solution.py:130
  500.3 1.2 copy-start.2
  553.4 105.4 %all-gather.6.cloned.1.call-start = ((), (), s32[]{:S(2)}) async-start(), calls=%async_computation.5 | async-start | bytes 5242880 | tf_op jit(solution)/shard_map/all_gather | solution.py:146
  557.9 130.9 %all-gather.8.cloned.1.call-start = ((), (), s32[]{:S(2)}) async-start(), calls=%async_computation.6 | async-start | bytes 1179648 | tf_op jit(solution)/shard_map/all_gather | solution.py:85
  658.7 4.6 copy-start.4
  663.4 3.2 copy-start.7
  663.4 3.2 copy-start.6
  663.4 35.1 %copy-start.5 = (bf16[1024,512]{1,0:T(8,128)(2,1)S(1)}, bf16[1024,512]{1,0:T(8,128)(2,1)}, u32[]{:S(2)}) copy-start(bf16[1024,512]{1,0:T(8,128)(2,1)} %all-gather.4.cloned.1.call-done) | copy-start | bytes 3145732
Sparse Core Ops, SparseCore 0:
  21.4 132.4 all-reduce.2
  220.4 147.5 reduce-scatter.1
  374.5 125.6 all-reduce.4
  553.5 22.4 all-gather.3
  578.0 80.7 all-gather.5
  666.7 22.0 all-gather.7

commit v2 on v1

--- a/solution.py
+++ b/solution.py
@@ -60,77 +60,332 @@
         return carry
     lax.fori_loop(0, n, panel, 0)
 
-def kernel(size, g_ref, u_ref, v_ref, mat):
+def log2(count):
+    return count.bit_length() - 1
+
+
+class Hypercube:
+    def __init__(self, seq_count, head_count):
+        self.seq = lax.axis_index("seq")
+        self.head = lax.axis_index("head")
+        self.seq_bits = [("seq", k) for k in range(log2(seq_count))]
+        self.head_bits = [("head", k) for k in range(log2(head_count))]
+        rest = self.seq_bits[1:] + self.head_bits
+        swapped = self.seq_bits[1:][::-1] + self.head_bits[::-1]
+        self.orders = [self.seq_bits[:1] + rest, self.seq_bits[:1] + swapped]
+
+    def bit(self, which):
+        axis, k = which
+        return (self.seq if axis == "seq" else self.head) // (1 << k) % 2
+
+    def partner(self, which):
+        axis, k = which
+        step = (1 - 2 * self.bit(which)) * (1 << k)
+        if axis == "seq":
+            return (self.seq + step, self.head)
+        return (self.seq, self.head + step)
+
+    def greet(self):
+        barrier = pltpu.get_barrier_semaphore()
+        bits = self.seq_bits + self.head_bits
+        for which in bits:
+            pl.semaphore_signal(
+                barrier, inc=1, device_id=self.partner(which), device_id_type=pl.DeviceIdType.MESH
+            )
+        pl.semaphore_wait(barrier, len(bits))
+
+    def copy(self, source, target, send_sem, recv_sem, which):
+        return pltpu.make_async_remote_copy(
+            src_ref=source,
+            dst_ref=target,
+            send_sem=send_sem,
+            recv_sem=recv_sem,
+            device_id=self.partner(which),
+            device_id_type=pl.DeviceIdType.MESH,
+        )
+
+
+def add_rows(target, start, source, offset, rows, columns):
+    step = min(rows, 64)
+
+    def add(i, carry):
+        t0 = pl.multiple_of(start + i * step, step)
+        s0 = pl.multiple_of(offset + i * step, step)
+        target[pl.ds(t0, step), columns] += source[pl.ds(s0, step), columns]
+        return carry
+
+    lax.fori_loop(0, rows // step, add, 0)
+
+
+def part_columns(width):
+    return [pl.ds(0, width // 2), pl.ds(width // 2, width // 2)]
+
+
+def halving_plan(rows, count):
+    plan, offset = [], 0
+    for _ in range(count):
+        split = rows >= 16
+        rows = rows // 2 if split else rows
+        plan.append((split, rows, offset))
+        offset += rows
+    return plan, offset
+
+
+def halve(cube, buf, recv, plan, send_sem, recv_sem):
+    columns = part_columns(buf.shape[1])
+    starts = [0, 0]
+    sent = []
+    for level, (split, rows, offset) in enumerate(plan):
+        copies = []
+        for part, order in enumerate(cube.orders):
+            which = order[level]
+            bit = cube.bit(which)
+            go = starts[part] + (1 - bit) * rows if split else starts[part]
+            if split:
+                starts[part] = starts[part] + bit * rows
+            copies.append(
+                cube.copy(
+                    buf.at[pl.ds(pl.multiple_of(go, 8), rows), columns[part]],
+                    recv.at[pl.ds(offset, rows), columns[part]],
+                    send_sem.at[level, part],
+                    recv_sem.at[level, part],
+                    which,
+                )
+            )
+        for copy in copies:
+            copy.start()
+        for part, copy in enumerate(copies):
+            copy.wait_recv()
+            if not split:
+                copy.wait_send()
+            else:
+                sent.append(copy)
+            add_rows(buf, starts[part], recv, offset, rows, columns[part])
+    for copy in sent:
+        copy.wait_send()
+    return starts
+
+
+def double(cube, buf, full, plan, starts, send_sem, recv_sem):
+    columns = part_columns(buf.shape[1])
+    rows = plan[-1][1]
+    for part in range(2):
+        here = pl.ds(pl.multiple_of(starts[part], 8), rows)
+        full[here, columns[part]] = buf[here, columns[part]]
+    starts = list(starts)
+    sent = []
+    for level in reversed(range(len(plan))):
+        split, rows, _ = plan[level]
+        if not split:
+            continue
+        copies = []
+        for part, order in enumerate(cube.orders):
+            which = order[level]
+            here = full.at[pl.ds(pl.multiple_of(starts[part], 8), rows), columns[part]]
+            copies.append(
+                cube.copy(here, here, send_sem.at[level, part], recv_sem.at[level, part], which)
+            )
+            starts[part] = starts[part] - cube.bit(which) * rows
+        for copy in copies:
+            copy.start()
+        for copy in copies:
+            copy.wait_recv()
+        sent += copies
+    for copy in sent:
+        copy.wait_send()
+
+
+def load_augmented(mat, full, size):
     r = lax.broadcasted_iota(jnp.int32, (size, size), 0)
     c = lax.broadcasted_iota(jnp.int32, (size, size), 1)
-    mat[:, :size] = g_ref[...]
+    mat[:, :size] = full[...]
     mat[:, size:] = (r == c).astype(jnp.float32)
+
+
+def upper_part(mat, size):
+    r = lax.broadcasted_iota(jnp.int32, (size, size), 0)
+    c = lax.broadcasted_iota(jnp.int32, (size, size), 1)
+    return jnp.where(c >= r, mat[:, :size], 0.0)
+
+
+def first_kernel(seq_count, head_count, g_ref, v_ref, buf, recv, full, mat, rs, rr, gs, gr):
+    size = g_ref.shape[0]
+    cube = Hypercube(seq_count, head_count)
+    cube.greet()
+    plan, _ = halving_plan(size, len(cube.orders[0]))
+    buf[...] = g_ref[...]
+    starts = halve(cube, buf, recv, plan, rs, rr)
+    double(cube, buf, full, plan, starts, gs, gr)
+    load_augmented(mat, full, size)
     factor(mat, size)
-    u_ref[...] = jnp.where(c >= r, mat[:, :size], 0.0)
     v_ref[...] = mat[:, size:]
 
-def chol_inv(g):
-    size = g.shape[0]
+
+def scratch_of(size, count):
+    _, total = halving_plan(size, count)
+    sems = pltpu.SemaphoreType.DMA((count, 2))
+    return [
+        pltpu.VMEM((size, size), jnp.float32),
+        pltpu.VMEM((total, size), jnp.float32),
+        pltpu.VMEM((size, size), jnp.float32),
+        pltpu.VMEM((size, 2 * size), jnp.float32),
+        sems,
+        sems,
+        sems,
+        sems,
+    ]
+
+
+def summed_inverse(gram, seq_count, head_count):
+    size = gram.shape[0]
     return pl.pallas_call(
-        functools.partial(kernel, size),
-        out_shape=[jax.ShapeDtypeStruct((size, size), jnp.float32)] * 2,
+        functools.partial(first_kernel, seq_count, head_count),
+        out_shape=jax.ShapeDtypeStruct((size, size), jnp.float32),
         in_specs=[pl.BlockSpec(memory_space=pltpu.VMEM)],
-        out_specs=[pl.BlockSpec(memory_space=pltpu.VMEM)] * 2,
-        scratch_shapes=[pltpu.VMEM((size, 2 * size), jnp.float32)],
-        compiler_params=pltpu.CompilerParams(vmem_limit_bytes=32 << 20),
-    )(g)
-
-
-def joined(part, axis, combine):
-    gathered = jax.tree.map(lambda a: lax.all_gather(a, axis), part)
-
-    def take(source):
-        return jax.tree.map(lambda a: lax.dynamic_index_in_dim(a, source, 0, False), gathered)
-
-    return lax.fori_loop(
-        1, lax.axis_size(axis), lambda source, state: combine(state, take(source)), take(0)
-    )
-
-
-def soft_join(former, latter):
-    joint_peak = jnp.maximum(former[0], latter[0])
-    former_factor = jnp.exp(former[0] - joint_peak)
-    latter_factor = jnp.exp(latter[0] - joint_peak)
-    return (
-        joint_peak,
-        former[1] * former_factor + latter[1] * latter_factor,
-        former[2] * former_factor[..., None] + latter[2] * latter_factor[..., None],
-    )
+        out_specs=pl.BlockSpec(memory_space=pltpu.VMEM),
+        scratch_shapes=scratch_of(size, log2(seq_count * head_count)),
+        compiler_params=pltpu.CompilerParams(
+            collective_id=0, has_side_effects=True, vmem_limit_bytes=24 << 20
+        ),
+        cost_estimate=pl.CostEstimate(
+            flops=100_000_000_000, bytes_accessed=4_000_000, transcendentals=0
+        ),
+    )(gram)
+
+
+def second_kernel(
+    seq_count, head_count, k_ref, o_ref, c_ref, u_ref, v_ref,
+    part_sum, part_recv, buf, recv, full, mat, rs, rr, gs, gr, cs, cr, as_, ar,
+):
+    size = o_ref.shape[1]
+    cube = Hypercube(seq_count, head_count)
+    cube.greet()
+    columns = part_columns(size)
+    width = k_ref.shape[1]
+    own = width // (seq_count * head_count)
+    count = len(cube.orders[0])
+    chunk = max(own, 128)
+    pieces = chunk // own
+
+    def place(block, order):
+        at = 0
+        for level, (axis, k) in enumerate(order):
+            bit = block // ((1 << k) * (1 if axis == "seq" else seq_count)) % 2
+            at = at + bit * (1 << (count - 1 - level))
+        return pl.multiple_of(at * own, own)
+
+    def product(index, carry):
+        c0 = pl.multiple_of(index * chunk, chunk)
+        value = lax.dot_general(
+            k_ref[:, pl.ds(c0, chunk)], o_ref[...], (((0,), (0,)), ((), ())),
+            preferred_element_type=jnp.float32,
+        )
+        for piece in range(pieces):
+            rows = value[piece * own:(piece + 1) * own]
+            for part, order in enumerate(cube.orders):
+                at = place(index * pieces + piece, order)
+                half = size // 2
+                part_sum[pl.ds(at, own), columns[part]] = rows[:, part * half:(part + 1) * half]
+        return carry
+
+    lax.fori_loop(0, width // chunk, product, 0)
+    plan, _ = halving_plan(width, count)
+    starts = halve(cube, part_sum, part_recv, plan, cs, cr)
+    mine = jnp.concatenate(
+        [
+            part_sum[pl.ds(pl.multiple_of(starts[part], own), own), columns[part]]
+            for part in range(2)
+        ],
+        axis=1,
+    )
+    buf[...] = lax.dot_general(
+        mine, mine, (((0,), (0,)), ((), ())), precision=HI, preferred_element_type=jnp.float32
+    )
+    plan, _ = halving_plan(size, count)
+    starts = halve(cube, buf, recv, plan, rs, rr)
+    double(cube, buf, full, plan, starts, gs, gr)
+    load_augmented(mat, full, size)
+    factor(mat, size)
+    u_ref[...] = upper_part(mat, size)
+    v_ref[...] = mat[:, size:]
+    c_ref[pl.ds(pl.multiple_of(cube.seq * own, own), own), :] = lax.dot_general(
+        mine, mat[:, size:], (((1,), (1,)), ((), ())), precision=HI,
+        preferred_element_type=jnp.float32,
+    ).astype(jnp.bfloat16)
+    held = [cube.seq]
+    sent = []
+    index = 0
+    for which in reversed(cube.seq_bits):
+        copies = []
+        for block in held:
+            here = c_ref.at[pl.ds(pl.multiple_of(block * own, own), own), :]
+            copies.append(cube.copy(here, here, as_.at[index], ar.at[index], which))
+            index += 1
+        for copy in copies:
+            copy.start()
+        for copy in copies:
+            copy.wait_recv()
+        sent += copies
+        step = (1 - 2 * cube.bit(which)) * (1 << which[1])
+        held = held + [block + step for block in held]
+    for copy in sent:
+        copy.wait_send()
+
+
+def coefficient_stage(keys, ortho, seq_count, head_count):
+    width = keys.shape[1]
+    size = ortho.shape[1]
+    count = log2(seq_count * head_count)
+    _, total = halving_plan(width, count)
+    sems = pltpu.SemaphoreType.DMA((count, 2))
+    more = pltpu.SemaphoreType.DMA((seq_count - 1,))
+    square = jax.ShapeDtypeStruct((size, size), jnp.float32)
+    vmem = pl.BlockSpec(memory_space=pltpu.VMEM)
+    return pl.pallas_call(
+        functools.partial(second_kernel, seq_count, head_count),
+        out_shape=[
+            jax.ShapeDtypeStruct((width // head_count, size), jnp.bfloat16), square, square,
+        ],
+        in_specs=[vmem] * 2,
+        out_specs=[vmem] * 3,
+        scratch_shapes=[
+            pltpu.VMEM((width, size), jnp.float32),
+            pltpu.VMEM((total, size), jnp.float32),
+        ]
+        + scratch_of(size, count)
+        + [sems, sems, more, more],
+        compiler_params=pltpu.CompilerParams(
+            collective_id=1, has_side_effects=True, vmem_limit_bytes=50 << 20
+        ),
+        cost_estimate=pl.CostEstimate(
+            flops=100_000_000_000, bytes_accessed=20_000_000, transcendentals=0
+        ),
+    )(keys, ortho)
 
 
 def per_device(cached_keys, sketch_matrix, cached_values, queries, new_keys, new_values):
     highest = lax.Precision.HIGHEST
     seq_count = lax.axis_size("seq")
     head_count = lax.axis_size("head")
-    tok_rows, key_width = cached_keys.shape
+    tok_rows = cached_keys.shape[0]
     sketch_rank = sketch_matrix.shape[1]
-    contract = (((0,), (0,)), ((), ()))
+    rows_with_rows = (((1,), (1,)), ((), ()))
     sketch = jnp.dot(cached_keys, sketch_matrix, preferred_element_type=jnp.float32)
-    gram_first = lax.psum(jnp.dot(sketch.T, sketch, precision=highest), ("seq", "head"))
-    _, inverse_first = chol_inv(gram_first)
-    rows_with_rows = (((1,), (1,)), ((), ()))
+    sketch_group = lax.all_gather(sketch, "head", axis=0, tiled=True)
+    gram_first = jnp.dot(sketch.T, sketch, precision=highest)
+    inverse_first = summed_inverse(gram_first, seq_count, head_count)
     orthonormal = lax.dot_general(sketch, inverse_first, rows_with_rows, precision=highest)
     stored_ortho = orthonormal.astype(jnp.bfloat16)
-    coef_rows = lax.psum_scatter(
-        lax.dot_general(cached_keys, stored_ortho, contract, preferred_element_type=jnp.float32),
-        ("head", "seq"),
-        scatter_dimension=0,
-        tiled=True,
-    )
-    gram_second = lax.psum(jnp.dot(coef_rows.T, coef_rows, precision=highest), ("seq", "head"))
-    upper_second, inverse_second = chol_inv(gram_second)
-    coef_piece = lax.dot_general(
-        coef_rows, inverse_second, rows_with_rows, precision=highest
+    coefficients, upper_second, inverse_second = coefficient_stage(
+        cached_keys, stored_ortho, seq_count, head_count
+    )
+    both = lax.dot_general(upper_second, inverse_first, (((1,), (0,)), ((), ())), precision=highest)
+    group_bases = lax.dot_general(
+        sketch_group, both, rows_with_rows, precision=highest
     ).astype(jnp.bfloat16)
-    coefficients = lax.all_gather(coef_piece, "seq", axis=0, tiled=True)
-    key_bases = lax.dot_general(
-        orthonormal, upper_second, rows_with_rows, precision=highest
-    ).astype(jnp.bfloat16)
+    key_bases = lax.dynamic_slice_in_dim(
+        group_bases, lax.axis_index("head") * tok_rows, tok_rows, 0
+    )
     heads_here, query_rows, head_dim = queries.shape
     rows_layer = STEPS * GQA
     score_scale = 1.0 / math.sqrt(head_dim)
@@ -143,7 +398,7 @@
     flat_queries = absorbed.reshape(heads_here * query_rows, sketch_rank)
     cache_scores = lax.dot_general(
         flat_queries,
-        lax.all_gather(key_bases, "head", axis=0, tiled=True),
+        group_bases,
         (((1,), (1,)), ((), ())),
         preferred_element_type=jnp.float32,
     )
@@ -155,14 +410,23 @@
     numerator = jnp.einsum(
         "klqn,nklh->klqh", weights_bf, value_view, preferred_element_type=jnp.float32
     ).reshape(heads_here, query_rows, head_dim)
-    row_peaks = local_peak.reshape(heads_here, query_rows)
-    totals = local_total.reshape(heads_here, query_rows)
     own_rows = query_rows // seq_count
     row_begin = lax.axis_index("seq") * own_rows
-    row_peaks, totals, numerator = joined((row_peaks, totals, numerator), "seq", soft_join)
-    row_peaks = lax.dynamic_slice_in_dim(row_peaks, row_begin, own_rows, 1)
-    totals = lax.dynamic_slice_in_dim(totals, row_begin, own_rows, 1)
-    numerator = lax.dynamic_slice_in_dim(numerator, row_begin, own_rows, 1)
+    packed = jnp.concatenate(
+        [
+            numerator,
+            jnp.broadcast_to(local_peak.reshape(heads_here, query_rows, 1), (heads_here, query_rows, 64)),
+            jnp.broadcast_to(local_total.reshape(heads_here, query_rows, 1), (heads_here, query_rows, 64)),
+        ],
+        axis=2,
+    )
+    packed = packed.reshape(heads_here, seq_count, own_rows, 2 * head_dim).transpose(1, 0, 2, 3)
+    packed = lax.all_to_all(packed, "seq", 0, 0)
+    part_peaks = packed[..., head_dim]
+    row_peaks = jnp.max(part_peaks, axis=0)
+    part_factor = jnp.exp(part_peaks - row_peaks)
+    totals = jnp.sum(part_factor * packed[..., head_dim + 64], axis=0)
+    numerator = jnp.sum(part_factor[..., None] * packed[..., :head_dim], axis=0)
     row_index = row_begin + jnp.arange(own_rows, dtype=jnp.int32)
     layer_of_row = row_index // rows_layer
     step_of_row = row_index // GQA % STEPS

time: 707 us -> 378 us (0.53)
  waiting for transfers between devices: 498 us -> 4.6 us
  Pallas kernels: 98.8 us -> 282 us
  blocking collectives: 17.7 us -> 0 us
    psum x2 -> x0, waiting for transfers between devices: 261 us -> none  [the longest x1 132 us: per_device(): lax.psum(jnp.dot(sketch.T, sketch, precision=highest), ('seq', 'head'))]
    pallas_call x2, Pallas kernels: 98.8 us -> 282 us  [the longest x1 184 us: coefficient_stage(): pl.pallas_call(functools.partial(second_kernel, seq_count, head_count), o...]
    reduce_scatter x1 -> x0, waiting for transfers between devices: 148 us -> none  [per_device(): lax.psum_scatter(lax.dot_general(cached_keys, stored_ortho, contract, pre...]
    all_gather x3 -> x1, waiting for transfers between devices: 88.8 us -> 0.01 us  [per_device(): sketch_group = lax.all_gather(sketch, 'head', axis=0, tiled=True)]
    all_gather x2 -> x0, blocking collectives: 17.7 us -> none  [joined(): gathered = jax.tree.map(lambda a: lax.all_gather(a, axis), part)]
    add x14 -> x0, other arithmetic: 7.67 us -> none  [the longest x7 7.49 us: soft_join(): former[2] * former_factor[..., None] + latter[2] * latter_factor[..., None]]
    dot_general x6 -> x4, matrix products: 28.7 us -> 27.7 us  [the longest x1 15.9 us: per_device(): lax.dot_general(sketch_group, both, rows_with_rows, precision=highest)]
  transfers between devices with their start and end apart: 6 -> 2, of which waited for: 6 -> 1; matrix products, arithmetic and copies ran while one was open for 3% -> 8% of each run, Pallas kernels for 0% -> 75%
where the time goes in v2:
time: 378 us
  Pallas kernels  282 us (75%)
  matrix products  50.5 us (13%)
  local copies, waits for them, and re-layouts  18.4 us (5%)
  between operations  14.3 us (4%)
  other arithmetic  5.03 us (1%)
  waiting for transfers between devices  4.6 us (1%)
    pallas_call x1, Pallas kernels, coefficient_stage(): pl.pallas_call(functools.partial(second_kernel, seq_count, head_count), o...  184 us
    pallas_call x1, Pallas kernels, summed_inverse(): pl.pallas_call(functools.partial(first_kernel, seq_count, head_count), ou...  97.2 us
    dot_general x1, matrix products, per_device(): lax.dot_general(sketch_group, both, rows_with_rows, precision=highest)  15.9 us
    reshape x1, local copies, waits for them, and re-layouts, per_device(): cached_values.reshape(cached_values.shape[0], heads_here, LAYERS, head_dim)  14.3 us
    dot_general x1, matrix products, per_device(): jnp.dot(cached_keys, sketch_matrix, preferred_element_type=jnp.float32)  10.4 us
  transfers between devices with their start and end apart: 2, of which 1 were waited for; matrix products, arithmetic and copies ran while one was open for 8% of the time, Pallas kernels for 75%

profile of v2, /device:TPU:0, one launch (start us, length us, event | category | flops | bytes accessed | tf_op | source)
XLA Modules:
  0.0 377.8 jit_solution(4585426643507785409)
XLA Ops:
  7.2 0.0 all-gather.2.cloned.1.call-start
  7.2 10.4 %fusion.20 = f32[1024,512]{1,0:T(8,128)} fusion(bf16[1024,4096]{1,0:T(8,128)(2,1)} %k_ref.1, bf16[4096,512]{1,0:T(8,128)(2,1)} %param.7), kind=kOutput, calls=%fused_computation.54 | convolution fusion | flops 4294967296 | bytes 14680064 | tf_op jit(solution)/shard_map/dot_general | solution.py:373
  17.7 5.7 %fusion.21.g_ref = f32[512,512]{1,0:T(8,128)S(1)} fusion(f32[1024,512]{1,0:T(8,128)} %fusion.20), kind=kOutput, calls=%fused_computation.55 | convolution fusion | flops 3221225472 | bytes 3145728 | tf_op jit(solution)/shard_map/dot_general | solution.py:375
  23.4 97.2 %shard_map.85 = f32[512,512]{1,0:T(8,128)S(1)} custom-call(f32[512,512]{1,0:T(8,128)S(1)} %fusion.21.g_ref), custom_call_target="tpu_custom_call" | custom-call | flops 99999997952 | bytes 4000000 | tf_op jit(solution)/shard_map/pallas_call | solution.py:241
  120.7 6.0 %convolution_convert_fusion.1.o_ref = bf16[1024,512]{1,0:T(8,128)(2,1)} fusion(f32[1024,512]{1,0:T(8,128)} %fusion.20, f32[512,512]{1,0:T(8,128)S(1)} %shard_map.85), kind=kOutput, calls=%fused_computation.6 | convolution fusion | flops 3221749760 | bytes 4194304 | tf_op jit(solution)/shard_map/dot_general | solution.py:377
  126.7 184.3 %shard_map.86 = (bf16[1024,512]{1,0:T(8,128)(2,1)S(1)}, f32[512,512]{1,0:T(8,128)S(1)}, f32[512,512]{1,0:T(8,128)}) custom-call(bf16[1024,4096]{1,0:T(8,128)(2,1)} %k_ref.1, bf16[1024,512]{1,0:T(8,128)(2,1)} %convolution_convert_fusion.1.o_ref), custom_call_target="tpu_custom_call" | custom-call | flops 99999997952 | bytes 20000000 | tf_op jit(solution)/shard_map/pallas_call | solution.py:344
  311.1 14.3 %reshape.177 = bf16[4096,2,4,128]{3,2,1,0:T(4,128)(2,1)} reshape(bf16[4096,1024]{1,0:T(8,128)(2,1)} %param.8) | data formatting | bytes 16777216 | tf_op jit(solution)/shard_map/reshape | solution.py:409
  325.4 0.1 fusion.5
  325.6 0.1 multiply_reduce_fusion
  325.7 0.3 fusion.4
  325.9 2.8 fusion.22
  328.8 15.9 %convolution_convert_fusion = bf16[4096,512]{1,0:T(8,128)(2,1)S(1)} fusion(f32[4096,512]{1,0:T(8,128)} %all-gather.2.cloned.1.call-done, f32[512,512]{1,0:T(8,128)} %fusion.22), kind=kOutput, calls=%fused_computation.2 | convolution fusion | flops 12886999040 | bytes 13631488 | tf_op jit(solution)/shard_map/dot_general | solution.py:383
  344.7 3.2 fusion.19
  348.0 0.1 broadcast_in_dim.16
  348.1 3.0 fusion.3
  351.0 0.1 broadcast_in_dim.18
  351.1 5.9 %fusion = f32[2,4,32,128]{3,2,1,0:T(8,128)S(1)} fusion(bf16[2,4,32,4096]{3,2,1,0:T(8,128)(2,1)S(1)} %bitcast.50, bf16[4096,2,4,128]{3,2,1,0:T(4,128)(2,1)} %reshape.177), kind=kOutput, calls=%fused_computation | convolution fusion | flops 268435456 | bytes 10616832 | tf_op jit(solution)/shard_map/klqn,nklh->klqh/dot_general | solution.py:410
  357.0 0.1 broadcast_in_dim.23
  357.1 0.1 broadcast_in_dim.17
  357.2 0.8 copy_bitcast_fusion
  358.0 3.4 all-to-all-start
  361.5 2.3 constant_dynamic-slice_fusion
  363.7 4.6 %all-to-all-done = f32[8,2,16,256]{3,2,1,0:T(8,128)S(1)} async-done(((f32[8,2,16,256]{3,2,1,0:T(8,128)}), f32[8,2,16,256]{3,2,1,0:T(8,128)S(1)}, u32[]{:S(2)}, u32[]{:S(2)}) %all-to-all-start) | async-done | bytes 262176 | tf_op jit(solution)/shard_map/all_to_all | solution.py:424
  368.3 0.1 fusion.18
  368.4 0.2 copy.45
  368.6 0.2 copy.44
  368.9 0.1 fusion.6
  369.0 0.1 copy.43
  369.1 0.1 copy.37
  369.2 0.1 multiply_reduce_fusion.1
  369.3 0.7 divide_convert_fusion
  370.0 1.0 copy.57
  (26 shorter events, 0.2 us)
Async XLA Ops:
  7.2 318.2 %copy-start = (bf16[2,128,128]{2,1,0:T(8,128)(2,1)S(1)}, bf16[2,128,128]{2,1,0:T(8,128)(2,1)}, u32[]{:S(2)}) copy-start(bf16[2,128,128]{2,1,0:T(8,128)(2,1)} %param.9) | copy-start | bytes 196612
  7.2 321.6 %all-gather.2.cloned.1.call-start = ((), (), s32[]{:S(2)}) async-start(), calls=%async_computation.1 | async-start | bytes 10485760 | tf_op jit(solution)/shard_map/all_gather | solution.py:374
  23.4 97.3 %copy-start.3 = (bf16[4,1024]{1,0:T(4,128)(2,1)S(1)}, bf16[4,1024]{1,0:T(4,128)(2,1)}, u32[]{:S(2)}) copy-start(bf16[4,1024]{1,0:T(4,128)(2,1)} %param.10) | copy-start | bytes 24580
  23.4 97.3 %copy-start.2 = (bf16[4,1024]{1,0:T(4,128)(2,1)S(1)}, bf16[4,1024]{1,0:T(4,128)(2,1)}, u32[]{:S(2)}) copy-start(bf16[4,1024]{1,0:T(4,128)(2,1)} %param.11) | copy-start | bytes 24580
  344.7 3.3 copy-start.1
  358.0 10.3 %all-to-all-start = ((f32[8,2,16,256]{3,2,1,0:T(8,128)}), f32[8,2,16,256]{3,2,1,0:T(8,128)S(1)}, u32[]{:S(2)}, u32[]{:S(2)}) async-start(f32[8,2,16,256]{3,2,1,0:T(8,128)} %copy_bitcast_fusion), calls=%async_computation | async-start | bytes 524288 | tf_op jit(solution)/shard_map/all_to_all | solution.py:424
Sparse Core Ops, SparseCore 0:
  17.8 156.5 all-gather.1

commit v3 on v2

--- a/solution.py
+++ b/solution.py
@@ -20,25 +20,46 @@
     lane = lax.broadcasted_iota(jnp.int32, (8, BLK), 1)
     s = [square[8 * g:8 * g + 8, :] for g in range(groups)]
     w = [(lane == sub + 8 * g).astype(jnp.float32) for g in range(groups)]
-    for j in range(BLK):
-        gj, r = divmod(j, 8)
-        row = s[gj][r:r + 1, :]
-        inv = 1.0 / jnp.broadcast_to(row[:, j:j + 1], (1, BLK))
-        srow = jnp.broadcast_to(row * inv, (8, BLK))
-        wrow = jnp.broadcast_to(w[gj][r:r + 1, :] * inv, (8, BLK))
-        for g in range(gj, groups):
-            if g == gj and r == 7:
-                continue
-            col = jnp.broadcast_to(s[g][:, j:j + 1], (8, BLK))
-            if g == gj:
-                col = jnp.where(sub > r, col, 0.0)
-            s[g] = s[g] - col * srow
-            w[g] = w[g] - col * wrow
+
+    def spread_row(value, p):
+        return jnp.broadcast_to(value[p:p + 1, :], (8, BLK))
+
+    def spread_column(value, j):
+        return jnp.broadcast_to(value[:, j:j + 1], (8, BLK))
+
     out = []
     for g in range(groups):
-        diag = jnp.sum(jnp.where(lane == sub + 8 * g, s[g], 0.0), axis=1, keepdims=True)
-        out.append(w[g] * lax.rsqrt(diag))
+        diag = [spread_column(s[g], 8 * g + q) for q in range(8)]
+        below = [[spread_column(s[h], 8 * g + q) for q in range(8)] for h in range(g + 1, groups)]
+        xs, xw = s[g], w[g]
+        forward = jnp.zeros((8, BLK), jnp.float32)
+        pivots = jnp.ones((8, BLK), jnp.float32)
+        for p in range(8):
+            pivot = spread_row(diag[p], p)
+            factor_of = jnp.where(sub == p, 0.0, diag[p] * (1.0 / pivot))
+            forward = jnp.where(sub == p, xw, forward)
+            pivots = jnp.where(sub == p, pivot, pivots)
+            for q in range(p + 1, 8):
+                diag[q] = diag[q] - factor_of * spread_row(diag[q], p)
+            xs = xs - factor_of * spread_row(xs, p)
+            xw = xw - factor_of * spread_row(xw, p)
+        out.append(forward * lax.rsqrt(pivots))
+        if g + 1 == groups:
+            continue
+        scale = 1.0 / pivots
+        xs, xw = xs * scale, xw * scale
+        rows_s = [spread_row(xs, q) for q in range(8)]
+        rows_w = [spread_row(xw, q) for q in range(8)]
+        for i, h in enumerate(range(g + 1, groups)):
+            change_s = [below[i][q] * rows_s[q] for q in range(8)]
+            change_w = [below[i][q] * rows_w[q] for q in range(8)]
+            while len(change_s) > 1:
+                change_s = [change_s[t] + change_s[t + 1] for t in range(0, len(change_s), 2)]
+                change_w = [change_w[t] + change_w[t + 1] for t in range(0, len(change_w), 2)]
+            s[h] = s[h] - change_s[0]
+            w[h] = w[h] - change_w[0]
     return jnp.concatenate(out, axis=0)
+
 
 def factor(mat, size):
     n = size // BLK
@@ -131,7 +152,7 @@
     return plan, offset
 
 
-def halve(cube, buf, recv, plan, send_sem, recv_sem):
+def halve(cube, buf, recv, plan, send_sem, recv_sem, meanwhile=None):
     columns = part_columns(buf.shape[1])
     starts = [0, 0]
     sent = []
@@ -154,6 +175,8 @@
             )
         for copy in copies:
             copy.start()
+        if level == 0 and meanwhile is not None:
+            meanwhile()
         for part, copy in enumerate(copies):
             copy.wait_recv()
             if not split:
@@ -288,9 +311,22 @@
                 part_sum[pl.ds(at, own), columns[part]] = rows[:, part * half:(part + 1) * half]
         return carry
 
-    lax.fori_loop(0, width // chunk, product, 0)
+    meanwhile = None
+    if pieces == 1:
+        core = cube.bit(cube.seq_bits[0])
+
+        def products_of(bit):
+            def step(index, carry):
+                return product(2 * index + bit, carry)
+
+            lax.fori_loop(0, width // chunk // 2, step, 0)
+
+        products_of(1 - core)
+        meanwhile = functools.partial(products_of, core)
+    else:
+        lax.fori_loop(0, width // chunk, product, 0)
     plan, _ = halving_plan(width, count)
-    starts = halve(cube, part_sum, part_recv, plan, cs, cr)
+    starts = halve(cube, part_sum, part_recv, plan, cs, cr, meanwhile)
     mine = jnp.concatenate(
         [
             part_sum[pl.ds(pl.multiple_of(starts[part], own), own), columns[part]]
@@ -405,10 +441,14 @@
     local_peak = jnp.max(cache_scores, axis=1)
     cache_weights = jnp.exp(cache_scores - local_peak[:, None])
     local_total = jnp.sum(cache_weights, axis=1)
-    weights_bf = cache_weights.astype(jnp.bfloat16).reshape(heads_here, LAYERS, rows_layer, -1)
-    value_view = cached_values.reshape(cached_values.shape[0], heads_here, LAYERS, head_dim)
-    numerator = jnp.einsum(
-        "klqn,nklh->klqh", weights_bf, value_view, preferred_element_type=jnp.float32
+    weights_bf = cache_weights.astype(jnp.bfloat16)
+    every = jnp.dot(weights_bf, cached_values, preferred_element_type=jnp.float32)
+    numerator = jnp.concatenate(
+        [
+            every[i * rows_layer:(i + 1) * rows_layer, i * head_dim:(i + 1) * head_dim]
+            for i in range(heads_here * LAYERS)
+        ],
+        axis=0,
     ).reshape(heads_here, query_rows, head_dim)
     own_rows = query_rows // seq_count
     row_begin = lax.axis_index("seq") * own_rows

time: 378 us -> 321 us (0.85)
  Pallas kernels: 282 us -> 238 us
  local copies, waits for them, and re-layouts: 18.4 us -> 4.58 us
    pallas_call x1, Pallas kernels: 97.2 us -> 73.4 us  [summed_inverse(): pl.pallas_call(functools.partial(first_kernel, seq_count, head_count), ou...]
    pallas_call x1, Pallas kernels: 184 us -> 165 us  [coefficient_stage(): pl.pallas_call(functools.partial(second_kernel, seq_count, head_count), o...]
    reshape x1 -> x0, local copies, waits for them, and re-layouts: 14.3 us -> none  [per_device(): cached_values.reshape(cached_values.shape[0], heads_here, LAYERS, head_dim)]
  transfers between devices with their start and end apart: 2 -> 2, of which waited for: 1 -> 1; matrix products, arithmetic and copies ran while one was open for 8% -> 5% of each run, Pallas kernels for 75% -> 74%
where the time goes in v3:
time: 321 us
  Pallas kernels  238 us (74%)
  matrix products  50.7 us (16%)
  between operations  14.3 us (4%)
  other arithmetic  5.1 us (2%)
  waiting for transfers between devices  4.6 us (1%)
  local copies, waits for them, and re-layouts  4.58 us (1%)
  starting transfers between devices  3.45 us (1%)
    pallas_call x1, Pallas kernels, coefficient_stage(): pl.pallas_call(functools.partial(second_kernel, seq_count, head_count), o...  165 us
    pallas_call x1, Pallas kernels, summed_inverse(): pl.pallas_call(functools.partial(first_kernel, seq_count, head_count), ou...  73.4 us
    dot_general x1, matrix products, per_device(): lax.dot_general(sketch_group, both, rows_with_rows, precision=highest)  16.2 us
    dot_general x1, matrix products, per_device(): jnp.dot(cached_keys, sketch_matrix, preferred_element_type=jnp.float32)  10.5 us
  transfers between devices with their start and end apart: 2, of which 1 were waited for; matrix products, arithmetic and copies ran while one was open for 5% of the time, Pallas kernels for 74%

profile of v3, /device:TPU:0, one launch (start us, length us, event | category | flops | bytes accessed | tf_op | source)
XLA Modules:
  0.0 321.2 jit_solution(2929261151681850606)
XLA Ops:
  7.2 0.0 all-gather.2.cloned.1.call-start
  7.2 10.5 %fusion.21 = f32[1024,512]{1,0:T(8,128)} fusion(bf16[1024,4096]{1,0:T(8,128)(2,1)} %k_ref.1, bf16[4096,512]{1,0:T(8,128)(2,1)} %param.7), kind=kOutput, calls=%fused_computation.62 | convolution fusion | flops 4294967296 | bytes 14680064 | tf_op jit(solution)/shard_map/dot_general | solution.py:409
  17.7 5.8 %fusion.22.g_ref = f32[512,512]{1,0:T(8,128)S(1)} fusion(f32[1024,512]{1,0:T(8,128)} %fusion.21), kind=kOutput, calls=%fused_computation.63 | convolution fusion | flops 3221225472 | bytes 3145728 | tf_op jit(solution)/shard_map/dot_general | solution.py:411
  23.5 73.4 %shard_map.85 = f32[512,512]{1,0:T(8,128)S(1)} custom-call(f32[512,512]{1,0:T(8,128)S(1)} %fusion.22.g_ref), custom_call_target="tpu_custom_call" | custom-call | flops 99999997952 | bytes 4000000 | tf_op jit(solution)/shard_map/pallas_call | solution.py:264
  97.0 6.1 %convolution_convert_fusion.1.o_ref = bf16[1024,512]{1,0:T(8,128)(2,1)} fusion(f32[1024,512]{1,0:T(8,128)} %fusion.21, f32[512,512]{1,0:T(8,128)S(1)} %shard_map.85), kind=kOutput, calls=%fused_computation.6 | convolution fusion | flops 3221749760 | bytes 4194304 | tf_op jit(solution)/shard_map/dot_general | solution.py:413
  103.0 164.9 %shard_map.86 = (bf16[1024,512]{1,0:T(8,128)(2,1)S(1)}, f32[512,512]{1,0:T(8,128)S(1)}, f32[512,512]{1,0:T(8,128)}) custom-call(bf16[1024,4096]{1,0:T(8,128)(2,1)} %k_ref.1, bf16[1024,512]{1,0:T(8,128)(2,1)} %convolution_convert_fusion.1.o_ref), custom_call_target="tpu_custom_call" | custom-call | flops 99999997952 | bytes 20000000 | tf_op jit(solution)/shard_map/pallas_call | solution.py:380
  268.1 0.1 fusion.6
  268.2 0.1 multiply_reduce_fusion
  268.3 0.3 fusion.5
  268.6 2.8 fusion.23
  271.4 16.2 %convolution_convert_fusion = bf16[4096,512]{1,0:T(8,128)(2,1)S(1)} fusion(f32[4096,512]{1,0:T(8,128)} %all-gather.2.cloned.1.call-done, f32[512,512]{1,0:T(8,128)} %fusion.23), kind=kOutput, calls=%fused_computation | convolution fusion | flops 12886999040 | bytes 13631488 | tf_op jit(solution)/shard_map/dot_general | solution.py:419
  287.6 3.3 %fusion.20 = (f32[256]{0:T(256)S(1)}, f32[256,4096]{1,0:T(8,128)}) fusion(bf16[256,512]{1,0:T(8,128)(2,1)S(1)} %bitcast.49, bf16[4096,512]{1,0:T(8,128)(2,1)S(1)} %convolution_convert_fusion), kind=kOutput, calls=%fused_computation.61 | convolution fusion | flops 1074790144 | bytes 8651776 | tf_op jit(solution)/shard_map/dot_general | solution.py:435
  290.9 0.1 broadcast_in_dim.16
  291.0 3.0 fusion
  294.0 0.4 copy-done.2
  294.4 5.8 %fusion.2 = f32[256,1024]{1,0:T(8,128)S(1)} fusion(bf16[4096,1024]{1,0:T(8,128)(2,1)} %param.8, f32[256,4096]{1,0:T(8,128)S(1)} %copy-done.2, f32[256]{0:T(256)S(1)} %get-tuple-element.20), kind=kOutput, calls=%fused_computation.4 | convolution fusion | flops 2149580800 | bytes 13632512 | tf_op jit(solution)/shard_map/dot_general | solution.py:445
  300.3 0.1 broadcast_in_dim.18
  300.4 0.1 broadcast_in_dim.23
  300.5 0.1 broadcast_in_dim.17
  300.6 0.8 copy_bitcast_fusion
  301.4 3.4 %all-to-all-start = ((f32[8,2,16,256]{3,2,1,0:T(8,128)}), f32[8,2,16,256]{3,2,1,0:T(8,128)S(1)}, u32[]{:S(2)}, u32[]{:S(2)}) async-start(f32[8,2,16,256]{3,2,1,0:T(8,128)} %copy_bitcast_fusion), calls=%async_computation | async-start | bytes 524288 | tf_op jit(solution)/shard_map/all_to_all | solution.py:464
  304.8 2.3 constant_dynamic-slice_fusion
  307.1 4.6 %all-to-all-done = f32[8,2,16,256]{3,2,1,0:T(8,128)S(1)} async-done(((f32[8,2,16,256]{3,2,1,0:T(8,128)}), f32[8,2,16,256]{3,2,1,0:T(8,128)S(1)}, u32[]{:S(2)}, u32[]{:S(2)}) %all-to-all-start) | async-done | bytes 262176 | tf_op jit(solution)/shard_map/all_to_all | solution.py:464
  311.7 0.1 fusion.19
  311.8 0.2 copy.40
  312.0 0.2 copy.41
  312.2 0.1 fusion.7
  312.3 0.1 copy.39
  312.5 0.1 copy.33
  312.6 0.1 multiply_reduce_fusion.1
  312.7 0.7 divide_convert_fusion
  313.4 1.0 copy.58
  (35 shorter events, 0.3 us)
Async XLA Ops:
  7.2 260.9 %copy-start = (bf16[2,128,128]{2,1,0:T(8,128)(2,1)S(1)}, bf16[2,128,128]{2,1,0:T(8,128)(2,1)}, u32[]{:S(2)}) copy-start(bf16[2,128,128]{2,1,0:T(8,128)(2,1)} %param.9) | copy-start | bytes 196612
  7.2 264.2 %all-gather.2.cloned.1.call-start = ((), (), s32[]{:S(2)}) async-start(), calls=%async_computation.1 | async-start | bytes 10485760 | tf_op jit(solution)/shard_map/all_gather | solution.py:410
  23.5 73.5 %copy-start.4 = (bf16[4,1024]{1,0:T(4,128)(2,1)S(1)}, bf16[4,1024]{1,0:T(4,128)(2,1)}, u32[]{:S(2)}) copy-start(bf16[4,1024]{1,0:T(4,128)(2,1)} %param.10) | copy-start | bytes 24580
  23.5 73.5 %copy-start.3 = (bf16[4,1024]{1,0:T(4,128)(2,1)S(1)}, bf16[4,1024]{1,0:T(4,128)(2,1)}, u32[]{:S(2)}) copy-start(bf16[4,1024]{1,0:T(4,128)(2,1)} %param.11) | copy-start | bytes 24580
  287.6 3.3 %copy-start.1 = (bf16[4096,512]{1,0:T(8,128)(2,1)}, bf16[4096,512]{1,0:T(8,128)(2,1)S(1)}, u32[]{:S(2)}) copy-start(bf16[4096,512]{1,0:T(8,128)(2,1)S(1)} %convolution_convert_fusion) | copy-start | bytes 12582916
  291.0 3.5 %copy-start.2 = (f32[256,4096]{1,0:T(8,128)S(1)}, f32[256,4096]{1,0:T(8,128)}, u32[]{:S(2)}) copy-start(f32[256,4096]{1,0:T(8,128)} %get-tuple-element.21) | copy-start | bytes 12582916
  301.4 10.3 %all-to-all-start = ((f32[8,2,16,256]{3,2,1,0:T(8,128)}), f32[8,2,16,256]{3,2,1,0:T(8,128)S(1)}, u32[]{:S(2)}, u32[]{:S(2)}) async-start(f32[8,2,16,256]{3,2,1,0:T(8,128)} %copy_bitcast_fusion), calls=%async_computation | async-start | bytes 524288 | tf_op jit(solution)/shard_map/all_to_all | solution.py:464
Sparse Core Ops, SparseCore 0:
  17.8 164.4 all-gather.1
